TPU v7x, 32 devices: a whole 2x2x4 slice. The times are simulated.
32 devices in a mesh: grp: 2 (over x), mem: 16 (over z, y, core).
Axes of the slice: x: 2, y: 2, z: 4, core: 2. Of those that a mesh axis runs over, the one named last changes fastest.
Arguments:
- state_ens: bfloat16 [512, 16384], P('mem', 'grp'), may hold values from -6 to 6
- obs_ens: bfloat16 [512, 32768], P('mem', 'grp'), may hold values from -6 to 6
- obs_value: float32 [32768], P(('grp', 'mem')), may hold values from -12 to 12
- obs_class: int32 [32768], P(('grp', 'mem')), may hold values from 0 to 15
- loc_table: bfloat16 [16], replicated, may hold values from 0.049804688 to 1
- nbr_weight: float32 [4], replicated, may hold values from 0.25 to 1
Outputs:
- analysis: bfloat16 [512, 16384], P('mem', 'grp')
All inputs are finite; a program needn't handle non-finite values.
Results may differ from a plain program's by a relative error of at most 0.0065.
Values may be sent and summed in bfloat16 or wider, within the bound.
A program may use at most 64 MiB of HBM per device.

v0:
```python
import jax
import jax.numpy as jnp
from jax import lax
from jax.sharding import PartitionSpec as P

MEMBERS = 512
SWEEPS = 5
ROW_PATCHES = 8


def shifted(array, axis, by):
    devices = lax.axis_size(axis)
    pairs = [(i, i + by) for i in range(devices) if 0 <= i + by < devices]
    return lax.ppermute(array, axis, pairs)


def lookup(classes, weight_table):
    codes = lax.broadcasted_iota(jnp.int32, (weight_table.shape[0], classes.shape[0]), 0)
    picked = jnp.where(codes == classes[None, :], weight_table.astype(jnp.float32)[:, None], 0.0)
    return jnp.sum(picked, axis=0).astype(jnp.bfloat16)


def mirror(product):
    return jnp.triu(product) + jnp.triu(product, 1).T


def obs_terms(obs_block, observed, classes, weight_table):
    centre = jnp.sum(obs_block, axis=0, dtype=jnp.float32) / obs_block.shape[0]
    spread = (obs_block.astype(jnp.float32) - centre).astype(jnp.bfloat16)
    rates = lookup(classes, weight_table)
    innovation = (rates.astype(jnp.float32) * (observed - centre)).astype(jnp.bfloat16)
    return (spread, rates, innovation)


def gram_terms(spread, rates, innovation):
    scaled = (spread.astype(jnp.float32) * rates.astype(jnp.float32)).astype(jnp.bfloat16)
    gram_part = lax.dot_general(
        spread, scaled, (((1,), (1,)), ((), ())), preferred_element_type=jnp.float32
    )
    vector_part = jnp.dot(spread, innovation, preferred_element_type=jnp.float32)
    return (mirror(gram_part), vector_part)


def newton_root(system):
    norm_total = jnp.sqrt(jnp.sum(system * system))
    identity = jnp.eye(system.shape[0], dtype=jnp.float32)
    iterate = system / norm_total
    root_inv = identity
    for sweep in range(SWEEPS):
        middle = 1.5 * identity - 0.5 * jnp.dot(root_inv, iterate, precision=lax.Precision.HIGHEST)
        iterate = jnp.dot(iterate, middle, precision=lax.Precision.HIGHEST)
        root_inv = jnp.dot(middle, root_inv, precision=lax.Precision.HIGHEST)
    return (root_inv, norm_total)


def shards(state_ens, obs_ens, obs_value, obs_class, loc_table, nbr_weight):
    state_patch, obs_patch = (
        lax.all_to_all(state_ens, "mem", split_axis=1, concat_axis=0, tiled=True),
        lax.all_to_all(obs_ens, "mem", split_axis=1, concat_axis=0, tiled=True),
    )
    spread, rates, innovation = obs_terms(obs_patch, obs_value, obs_class, loc_table)
    gram_own, vector_own = gram_terms(spread, rates, innovation)
    position = lax.axis_index(("grp", "mem"))
    column = position % ROW_PATCHES
    west_open = (column != 0).astype(jnp.float32)
    east_open = (column != ROW_PATCHES - 1).astype(jnp.float32)
    system = gram_own + (MEMBERS - 1.0) * jnp.eye(MEMBERS, dtype=jnp.float32)
    rhs_vector = vector_own
    links = ((1, 0, west_open), (-1, 1, east_open), (ROW_PATCHES, 2, 1.0), (-ROW_PATCHES, 3, 1.0))
    for offset, direction, active in links:
        factor = nbr_weight[direction] * active
        gram_far, vector_far = shifted((gram_own, vector_own), ("grp", "mem"), offset)
        system = system + factor * gram_far
        rhs_vector = rhs_vector + factor * vector_far
    root_inv, norm_total = newton_root(system)
    half_step = jnp.dot(root_inv, rhs_vector, precision=lax.Precision.HIGHEST)
    mean_weight = jnp.dot(root_inv, half_step, precision=lax.Precision.HIGHEST) / norm_total
    transform = (jnp.sqrt((MEMBERS - 1.0) / norm_total) * root_inv + mean_weight[:, None]).astype(
        jnp.bfloat16
    )
    centre = jnp.sum(state_patch, axis=0, dtype=jnp.float32) / MEMBERS
    deviation = (state_patch.astype(jnp.float32) - centre).astype(jnp.bfloat16)
    update = lax.dot_general(
        transform, deviation, (((0,), (0,)), ((), ())), preferred_element_type=jnp.float32
    )
    analysis_patch = (centre + update).astype(jnp.bfloat16)
    return lax.all_to_all(analysis_patch, "mem", split_axis=0, concat_axis=1, tiled=True)


def solution(mesh):
    in_specs = (P("mem", "grp"), P("mem", "grp"), P(("grp", "mem")), P(("grp", "mem")), P(), P())
    out_specs = P("mem", "grp")
    return jax.shard_map(shards, mesh=mesh, in_specs=in_specs, out_specs=out_specs, check_vma=False)
```

profile of v0, /device:TPU:0, one launch (start us, length us, event | category | flops | bytes accessed | tf_op | source)
XLA Modules:
  0.0 228.9 jit_solution(17146093487934277856)
XLA Ops:
  0.0 2.3 copy.60
  2.3 7.5 %all-to-all-start.1 = ((bf16[32,16,1024]{2,0,1:T(8,128)(2,1)}), bf16[32,16,1024]{2,0,1:T(8,128)(2,1)S(1)}, u32[]{:S(2)}, u32[]{:S(2)}) async-start(bf16[32,16,1024]{2,0,1:T(8,128)(2,1)} %bitcast.74), calls=%async_computation.1 | async-start | bytes 2097152 | tf_op jit(solution)/shard_map/all_to_all | solution.py:59
  10.8 21.9 %all-to-all-done.1 = bf16[32,16,1024]{2,0,1:T(8,128)(2,1)S(1)} async-done(((bf16[32,16,1024]{2,0,1:T(8,128)(2,1)}), bf16[32,16,1024]{2,0,1:T(8,128)(2,1)S(1)}, u32[]{:S(2)}, u32[]{:S(2)}) %all-to-all-start.1) | async-done | bytes 1048608 | tf_op jit(solution)/shard_map/all_to_all | solution.py:59
  32.8 7.0 %all-to-all-start = ((bf16[32,16,512]{2,0,1:T(8,128)(2,1)}), bf16[32,16,512]{2,0,1:T(8,128)(2,1)S(1)}, u32[]{:S(2)}, u32[]{:S(2)}) async-start(bf16[32,16,512]{2,0,1:T(8,128)(2,1)} %bitcast.75), calls=%async_computation | async-start | bytes 1048576 | tf_op jit(solution)/shard_map/all_to_all | solution.py:58
  41.2 1.3 copy.43
  42.5 2.4 %fusion.3 = f32[512,512]{0,1:T(8,128)} fusion(f32[512,512]{1,0:T(8,128)S(1)} %fusion.9, f32[512,512]{0,1:T(8,128)} %copy.43, s32[512]{0:T(512)S(1)} %iota_add_fusion), kind=kLoop, calls=%fused_computation.21 | loop fusion | flops 1310720 | bytes 3147776 | tf_op jit(solution)/shard_map/add | solution.py:24
  44.9 1.3 collective-permute-start.3
  46.2 6.4 %collective-permute-start.2 = (f32[512,512]{0,1:T(8,128)}, f32[512,512]{0,1:T(8,128)}, u32[]{:S(2)}, u32[]{:S(2)}) collective-permute-start(f32[512,512]{0,1:T(8,128)} %fusion.3), channel_id=1, source_target_pairs={{0,8},{1,9},{2,10},{3,11},{4,12},{5,13},{6,14},{7,15},{8,16},{9,17... | collective-permute-start | bytes 3145736 | tf_op jit(solution)/shard_map/ppermute | solution.py:14
  52.6 1.3 collective-permute-start.1
  53.9 4.0 %collective-permute-start = (f32[512,512]{0,1:T(8,128)}, f32[512,512]{0,1:T(8,128)}, u32[]{:S(2)}, u32[]{:S(2)}) collective-permute-start(f32[512,512]{0,1:T(8,128)} %fusion.3), channel_id=1, source_target_pairs={{0,1},{1,2},{2,3},{3,4},{4,5},{5,6},{6,7},{7,8},{8,9},{9,10},{10,1... | collective-permute-start | bytes 3145736 | tf_op jit(solution)/shard_map/ppermute | solution.py:14
  58.6 1.3 collective-permute-start.7
  61.8 94.5 %collective-permute-done.7 = f32[512]{0:T(512)S(1)} collective-permute-done((f32[512]{0:T(512)S(1)}, f32[512]{0:T(512)S(1)}, u32[]{:S(2)}, u32[]{:S(2)}) %collective-permute-start.7) | collective-permute-done | bytes 2080 | tf_op jit(solution)/shard_map/ppermute | solution.py:14
  156.3 1.5 collective-permute-start.6
  159.1 1.3 collective-permute-start.5
  160.4 1.7 collective-permute-done.5
  162.1 3.8 %collective-permute-start.4 = (f32[512]{0:T(512)S(1)}, f32[512]{0:T(512)S(1)}, u32[]{:S(2)}, u32[]{:S(2)}) collective-permute-start(f32[512]{0:T(512)S(1)} %bitcast.85), channel_id=1, source_target_pairs={{0,1},{1,2},{2,3},{3,4},{4,5},{5,6},{6,7},{7,8},{8,9},{9,10},{10,1... | collective-permute-start | bytes 6152 | tf_op jit(solution)/shard_map/ppermute | solution.py:14
  166.5 1.2 multiply_add_fusion.1
  167.8 4.5 %multiply_reduce_fusion = (f32[]{:T(128)}, f32[512,512]{0,1:T(8,128)S(1)}) fusion(f32[512,512]{0,1:T(8,128)S(1)} %collective-permute-done.3, f32[]{:T(128)} %bitcast.7, f32[512,512]{0,1:T(8,128)} %collective-permute-done.2, f32[]{:T(128)} %bitcast.6, f32[512,512]{0,1:T(8,128)} %collective-permute-done.1, f32[]{:T(128)S(6)} %mul.122, ...), kind=kLoop, calls=%fused_computation.23 | loop fusion | flops 3407871 | bytes 6291476 | tf_op jit(solution)/shard_map/reduce_sum | solution.py:45
  174.0 3.5 %fusion.7 = f32[512,512]{1,0:T(8,128)S(1)} fusion(f32[512,512]{0,1:T(8,128)S(1)} %select_subtract_fusion.4, f32[512,512]{0,1:T(8,128)S(1)} %get-tuple-element.6, f32[]{:T(128)S(6)} %sqrt.6), kind=kOutput, calls=%fused_computation.34 | convolution fusion | flops 1610874880 | bytes 3145732 | tf_op jit(solution)/shard_map/dot_general | solution.py:51
  177.5 1.9 fusion.4
  179.4 1.9 select_subtract_fusion.3
  181.3 1.9 fusion.11
  183.1 2.1 fusion.10
  185.2 1.9 select_subtract_fusion.2
  187.1 1.9 fusion.13
  189.0 1.8 fusion.12
  190.9 1.9 select_subtract_fusion.1
  192.7 1.8 fusion.14
  194.6 2.1 fusion.15
  196.8 1.9 select_subtract_fusion
  198.7 1.8 fusion.16
  203.1 24.9 %all_to_all.45 = bf16[16,32,512]{2,1,0:T(8,128)(2,1)S(1)} all-to-all(bf16[16,32,512]{2,1,0:T(8,128)(2,1)S(1)} %bitcast.81), channel_id=1, replica_groups=mesh['grp'=2,'mem'=16] {'mem'}, dimensions={0} | all-to-all | bytes 1048576 | tf_op jit(solution)/shard_map/all_to_all | solution.py:87
  (39 shorter events, 9.9 us)
Async XLA Ops:
  2.3 7.5 %copy-start.4 = (bf16[16]{0:T(256)(128)(2,1)S(1)}, bf16[16]{0:T(256)(128)(2,1)}, u32[]{:S(2)}) copy-start(bf16[16]{0:T(256)(128)(2,1)} %param.10) | copy-start | bytes 100
  2.3 7.6 %copy-start.2 = (s32[1024]{0:T(1024)S(1)}, s32[1024]{0:T(1024)}, u32[]{:S(2)}) copy-start(s32[1024]{0:T(1024)} %param.9) | copy-start | bytes 12292
  2.3 7.7 %copy-start = (bf16[32,8192]{1,0:T(8,128)(2,1)S(1)}, bf16[32,8192]{1,0:T(8,128)(2,1)}, u32[]{:S(2)}) copy-start(bf16[32,8192]{1,0:T(8,128)(2,1)} %param.6) | copy-start | bytes 1572868
  2.3 30.5 %all-to-all-start.1 = ((bf16[32,16,1024]{2,0,1:T(8,128)(2,1)}), bf16[32,16,1024]{2,0,1:T(8,128)(2,1)S(1)}, u32[]{:S(2)}, u32[]{:S(2)}) async-start(bf16[32,16,1024]{2,0,1:T(8,128)(2,1)} %bitcast.74), calls=%async_computation.1 | async-start | bytes 2097152 | tf_op jit(solution)/shard_map/all_to_all | solution.py:59
  32.8 7.2 %copy-start.3 = (f32[1024]{0:T(1024)S(1)}, f32[1024]{0:T(1024)}, u32[]{:S(2)}) copy-start(f32[1024]{0:T(1024)} %param.8) | copy-start | bytes 12292
  32.8 125.0 %all-to-all-start = ((bf16[32,16,512]{2,0,1:T(8,128)(2,1)}), bf16[32,16,512]{2,0,1:T(8,128)(2,1)S(1)}, u32[]{:S(2)}, u32[]{:S(2)}) async-start(bf16[32,16,512]{2,0,1:T(8,128)(2,1)} %bitcast.75), calls=%async_computation | async-start | bytes 1048576 | tf_op jit(solution)/shard_map/all_to_all | solution.py:58
  44.9 122.9 %collective-permute-start.3 = (f32[512,512]{0,1:T(8,128)}, f32[512,512]{0,1:T(8,128)S(1)}, u32[]{:S(2)}, u32[]{:S(2)}) collective-permute-start(f32[512,512]{0,1:T(8,128)} %fusion.3), channel_id=1, source_target_pairs={{8,0},{9,1},{10,2},{11,3},{12,4},{13,5},{14,6},{15,7},{16,8},{17,9... | collective-permute-start | bytes 3145736 | tf_op jit(solution)/shard_map/ppermute | solution.py:14
  46.2 121.6 %collective-permute-start.2 = (f32[512,512]{0,1:T(8,128)}, f32[512,512]{0,1:T(8,128)}, u32[]{:S(2)}, u32[]{:S(2)}) collective-permute-start(f32[512,512]{0,1:T(8,128)} %fusion.3), channel_id=1, source_target_pairs={{0,8},{1,9},{2,10},{3,11},{4,12},{5,13},{6,14},{7,15},{8,16},{9,17... | collective-permute-start | bytes 3145736 | tf_op jit(solution)/shard_map/ppermute | solution.py:14
  52.6 115.2 %collective-permute-start.1 = (f32[512,512]{0,1:T(8,128)}, f32[512,512]{0,1:T(8,128)}, u32[]{:S(2)}, u32[]{:S(2)}) collective-permute-start(f32[512,512]{0,1:T(8,128)} %fusion.3), channel_id=1, source_target_pairs={{1,0},{2,1},{3,2},{4,3},{5,4},{6,5},{7,6},{8,7},{9,8},{10,9},{11,1... | collective-permute-start | bytes 3145736 | tf_op jit(solution)/shard_map/ppermute | solution.py:14
  53.9 113.9 %collective-permute-start = (f32[512,512]{0,1:T(8,128)}, f32[512,512]{0,1:T(8,128)}, u32[]{:S(2)}, u32[]{:S(2)}) collective-permute-start(f32[512,512]{0,1:T(8,128)} %fusion.3), channel_id=1, source_target_pairs={{0,1},{1,2},{2,3},{3,4},{4,5},{5,6},{6,7},{7,8},{8,9},{9,10},{10,1... | collective-permute-start | bytes 3145736 | tf_op jit(solution)/shard_map/ppermute | solution.py:14
  58.2 1.7 copy-start.1
  58.6 97.7 %collective-permute-start.7 = (f32[512]{0:T(512)S(1)}, f32[512]{0:T(512)S(1)}, u32[]{:S(2)}, u32[]{:S(2)}) collective-permute-start(f32[512]{0:T(512)S(1)} %bitcast.82), channel_id=1, source_target_pairs={{8,0},{9,1},{10,2},{11,3},{12,4},{13,5},{14,6},{15,7},{16,8},{17,9... | collective-permute-start | bytes 6152 | tf_op jit(solution)/shard_map/ppermute | solution.py:14
  156.3 2.8 %collective-permute-start.6 = (f32[512]{0:T(512)S(1)}, f32[512]{0:T(512)S(1)}, u32[]{:S(2)}, u32[]{:S(2)}) collective-permute-start(f32[512]{0:T(512)S(1)} %bitcast.83), channel_id=1, source_target_pairs={{0,8},{1,9},{2,10},{3,11},{4,12},{5,13},{6,14},{7,15},{8,16},{9,17... | collective-permute-start | bytes 6152 | tf_op jit(solution)/shard_map/ppermute | solution.py:14
  159.1 3.0 %collective-permute-start.5 = (f32[512]{0:T(512)S(1)}, f32[512]{0:T(512)S(1)}, u32[]{:S(2)}, u32[]{:S(2)}) collective-permute-start(f32[512]{0:T(512)S(1)} %bitcast.84), channel_id=1, source_target_pairs={{1,0},{2,1},{3,2},{4,3},{5,4},{6,5},{7,6},{8,7},{9,8},{10,9},{11,1... | collective-permute-start | bytes 6152 | tf_op jit(solution)/shard_map/ppermute | solution.py:14
  162.1 4.4 %collective-permute-start.4 = (f32[512]{0:T(512)S(1)}, f32[512]{0:T(512)S(1)}, u32[]{:S(2)}, u32[]{:S(2)}) collective-permute-start(f32[512]{0:T(512)S(1)} %bitcast.85), channel_id=1, source_target_pairs={{0,1},{1,2},{2,3},{3,4},{4,5},{5,6},{6,7},{7,8},{8,9},{9,10},{10,1... | collective-permute-start | bytes 6152 | tf_op jit(solution)/shard_map/ppermute | solution.py:14
where the time goes:
time: 230 us; the launch traced here: 229 us
  waiting for transfers between devices  120 us (52%)
  starting transfers between devices  35.4 us (15%)
  matrix products  31 us (13%)
  blocking collectives  24.9 us (11%)
  other arithmetic  9.38 us (4%)
  local copies, waits for them, and re-layouts  5.99 us (3%)
  between operations  2.39 us (1%)
    ppermute x8, waiting for transfers between devices, shifted(): return lax.ppermute(array, axis, pairs)  97.9 us
    all_to_all x1, blocking collectives, shards(): lax.all_to_all(analysis_patch, 'mem', split_axis=0, concat_axis=1, tiled=...  24.9 us
    all_to_all x1, waiting for transfers between devices, shards(): lax.all_to_all(obs_ens, 'mem', split_axis=1, concat_axis=0, tiled=True)  21.9 us
    ppermute x8, starting transfers between devices, shifted(): return lax.ppermute(array, axis, pairs)  20.9 us
    dot_general x5, matrix products, newton_root(): root_inv = jnp.dot(middle, root_inv, precision=lax.Precision.HIGHEST)  9.49 us
    dot_general x4, matrix products, newton_root(): iterate = jnp.dot(iterate, middle, precision=lax.Precision.HIGHEST)  9.33 us
    dot_general x5, matrix products, newton_root(): jnp.dot(root_inv, iterate, precision=lax.Precision.HIGHEST)  8.49 us
    all_to_all x1, starting transfers between devices, shards(): lax.all_to_all(obs_ens, 'mem', split_axis=1, concat_axis=0, tiled=True)  7.52 us
  transfers between devices with their start and end apart: 10, of which 5 were waited for; matrix products, arithmetic and copies ran while one was open for 4% of the time, Pallas kernels for 0%

commit v1 on v0

v1 whole, which is shorter than its diff:
```python
import functools
import jax
import jax.numpy as jnp
from jax import lax
from jax.experimental import pallas as pl
from jax.experimental.pallas import tpu as pltpu
from jax.sharding import PartitionSpec as P

SWEEPS = 5
ROW_PATCHES = 8
CORES = 2
BLOCK = 128
BF16 = jnp.bfloat16
F32 = jnp.float32
MESH = pl.DeviceIdType.MESH


class Grid:
    def __init__(self, groups, members):
        self.groups, self.members = groups, members
        self.rows = members // ROW_PATCHES
        self.slabs = ROW_PATCHES // CORES
        self.slab = members // self.slabs

    def split(self, mem):
        return mem // self.slab, (mem % self.slab) // CORES, mem % CORES

    def join(self, z, y, core):
        return z * self.slab + y * CORES + core

    def flip(self, group, row):
        return row + (group % 2) * (self.rows - 1 - 2 * row)

    def patch(self, group, mem):
        z, y, core = self.split(mem)
        return self.flip(group, y) * ROW_PATCHES + z * CORES + core

    def holder(self, group, patch):
        row, column = patch // ROW_PATCHES, patch % ROW_PATCHES
        return self.join(column // CORES, self.flip(group, row), column % CORES)

    def steps(self):
        order = [2, 1, 3, 0] if self.slabs == 4 else list(range(self.slabs))[::-1]
        return [
            (dz, [(dy, dc) for dy in range(self.rows) for dc in range(CORES) if (dz, dy, dc) != (0, 0, 0)])
            for dz in order
        ]

    def peer(self, mem, dz, dy, dc):
        z, y, core = self.split(mem)
        return self.join((z + dz) % self.slabs, (y + dy) % self.rows, (core + dc) % CORES)


def halves(value):
    high = value.astype(BF16)
    return high, (value - high.astype(F32)).astype(BF16)


def dot(a, b):
    return jnp.dot(a, b, preferred_element_type=F32)


def kernel(
    grid, weights, table, value_ref, class_ref, state_ref, obs_ref, out_ref,
    obs_in, state_in, value_in, class_in, spread, scaled, send, got, system,
    wh, wl, mh, ml, zh, zl, th, tl, ana,
    local_sems, meta_sems, obs_send, obs_recv, state_send, state_recv,
    gram_send, gram_recv, out_send, out_recv,
):
    group, mem = lax.axis_index("grp"), lax.axis_index("mem")
    members = system.shape[0]
    rows = obs_in.shape[1]
    wide, cells = obs_in.shape[2], state_in.shape[2]
    z, y, core = grid.split(mem)
    row, column = grid.flip(group, y), z * CORES + core
    all_row = group * grid.rows + row
    last_row = grid.groups * grid.rows - 1
    steps = grid.steps()
    flat = [(dz, dy, dc) for dz, inner in steps for dy, dc in inner]

    north_row, south_row = jnp.maximum(all_row - 1, 0), jnp.minimum(all_row + 1, last_row)
    north_group, south_group = north_row // grid.rows, south_row // grid.rows
    west, east = jnp.maximum(column - 1, 0), jnp.minimum(column + 1, ROW_PATCHES - 1)
    neighbours = (
        (column > 0, (group, grid.join(west // CORES, y, west % CORES))),
        (column < ROW_PATCHES - 1, (group, grid.join(east // CORES, y, east % CORES))),
        (all_row > 0, (north_group, grid.join(z, grid.flip(north_group, north_row % grid.rows), core))),
        (all_row < last_row, (south_group, grid.join(z, grid.flip(south_group, south_row % grid.rows), core))),
    )

    barrier = pltpu.get_barrier_semaphore()
    for step in flat:
        pl.semaphore_signal(barrier, inc=1, device_id=(group, grid.peer(mem, *step)), device_id_type=MESH)
    for there, far in ((north_group, neighbours[2][1]), (south_group, neighbours[3][1])):

        @pl.when(there != group)
        def _():
            pl.semaphore_signal(barrier, inc=1, device_id=far, device_id_type=MESH)

    outside = (all_row - north_row) * (group - north_group) + (south_row - all_row) * (south_group - group)
    pl.semaphore_wait(barrier, len(flat) + outside)

    def columns_of(device, width):
        return pl.ds(pl.multiple_of(grid.patch(group, device) * width, BLOCK), width)

    def obs_copy(k):
        to = grid.peer(mem, *flat[k])
        return pltpu.make_async_remote_copy(
            src_ref=obs_ref.at[:, columns_of(to, wide)], dst_ref=obs_in.at[mem],
            send_sem=obs_send.at[k], recv_sem=obs_recv.at[k], device_id=(group, to), device_id_type=MESH)

    def state_copy(k):
        to = grid.peer(mem, *flat[k])
        return pltpu.make_async_remote_copy(
            src_ref=state_ref.at[:, columns_of(to, cells)], dst_ref=state_in.at[mem],
            send_sem=state_send.at[k], recv_sem=state_recv.at[k], device_id=(group, to), device_id_type=MESH)

    def out_copy(k):
        to = grid.peer(mem, *flat[k])
        return pltpu.make_async_remote_copy(
            src_ref=ana.at[to], dst_ref=out_ref.at[:, columns_of(mem, cells)],
            send_sem=out_send.at[k], recv_sem=out_recv.at[k], device_id=(group, to), device_id_type=MESH)

    meta_to = grid.holder(group, mem)
    meta_pairs = ((value_ref, value_in), (class_ref, class_in))

    def meta_copy(k):
        return pltpu.make_async_remote_copy(
            src_ref=meta_pairs[k][0], dst_ref=meta_pairs[k][1], send_sem=meta_sems.at[0, k],
            recv_sem=meta_sems.at[1, k], device_id=(group, meta_to), device_id_type=MESH)

    def meta_local(k):
        return pltpu.make_async_copy(meta_pairs[k][0], meta_pairs[k][1], meta_sems.at[1, k])

    @pl.when(meta_to != mem)
    def _():
        for k in range(2):
            meta_copy(k).start()

    @pl.when(meta_to == mem)
    def _():
        for k in range(2):
            meta_local(k).start()

    own_obs = pltpu.make_async_copy(obs_ref.at[:, columns_of(mem, wide)], obs_in.at[mem], local_sems.at[0])
    own_state = pltpu.make_async_copy(state_ref.at[:, columns_of(mem, cells)], state_in.at[mem], local_sems.at[1])
    for k in range(len(flat)):
        obs_copy(k).start()
    own_obs.start()
    own_state.start()

    @pl.when(meta_to != mem)
    def _():
        for k in range(2):
            meta_copy(k).wait()

    @pl.when(meta_to == mem)
    def _():
        for k in range(2):
            meta_local(k).wait()

    rates = jnp.zeros(class_in.shape, F32)
    for code in range(table.shape[0]):
        rates = jnp.where(class_in[...] == code, table[code], rates)

    own_obs.wait()
    for k in range(len(flat)):
        obs_copy(k).wait_recv()

    def add_up(source, width):
        def body(i, total):
            return total + jnp.sum(source[i].astype(F32), axis=0, keepdims=True)

        return lax.fori_loop(0, grid.members, body, jnp.zeros((1, width), F32)) / members

    centre = add_up(obs_in, wide)

    def spread_body(i, carry):
        block = (obs_in[i].astype(F32) - centre).astype(BF16)
        spread[i] = block
        scaled[i] = (block.astype(F32) * rates).astype(BF16)
        return carry

    lax.fori_loop(0, grid.members, spread_body, 0)
    innovation = (rates * (value_in[...] - centre)).astype(BF16)

    blocks = members // BLOCK
    pairs = [(i, j) for i in range(blocks) for j in range(i, blocks)]
    all_spread = spread[...].reshape(members, wide)
    all_scaled = scaled[...].reshape(members, wide)
    vector = lax.dot_general(
        jnp.broadcast_to(innovation, (16, wide)), all_spread, (((1,), (1,)), ((), ())), preferred_element_type=F32)[:1]
    pieces = jnp.concatenate(
        [vector[:, b * BLOCK:(b + 1) * BLOCK] for b in range(blocks)]
        + [jnp.zeros((8 - blocks, BLOCK), F32)], axis=0)
    pieces_high = pieces.astype(BF16).astype(F32)
    tail = len(pairs) * BLOCK
    send[tail:tail + 16, :] = jnp.concatenate([pieces_high, pieces - pieces_high], axis=0).astype(BF16)
    part = 2 * BLOCK
    for start in range(0, members, part):
        stripe = lax.dot_general(
            all_spread[start:start + part], all_scaled[start:], (((1,), (1,)), ((), ())), preferred_element_type=F32)
        system[start:start + part, start:] = stripe
        for index, (i, j) in enumerate(pairs):
            if start <= i * BLOCK < start + part:
                at = i * BLOCK - start
                piece = stripe[at:at + BLOCK, j * BLOCK - start:(j + 1) * BLOCK - start]
                send[index * BLOCK:(index + 1) * BLOCK, :] = piece.astype(BF16)

    opposite = (1, 0, 3, 2)

    def gram_copy(d):
        return pltpu.make_async_remote_copy(
            src_ref=send, dst_ref=got.at[opposite[d]], send_sem=gram_send.at[d],
            recv_sem=gram_recv.at[opposite[d]], device_id=neighbours[d][1], device_id_type=MESH)

    def gram_arrival(d):
        return pltpu.make_async_remote_copy(
            src_ref=send, dst_ref=got.at[d], send_sem=gram_send.at[d],
            recv_sem=gram_recv.at[d], device_id=neighbours[d][1], device_id_type=MESH)

    for d in (2, 3, 0, 1):

        @pl.when(neighbours[d][0])
        def _():
            gram_copy(d).start()

    for k in range(len(flat)):
        state_copy(k).start()

    rhs_ref = value_in
    rhs_ref[:, :members] = vector
    for d in (0, 1, 2, 3):

        @pl.when(neighbours[d][0])
        def _():
            gram_arrival(d).wait_recv()
            factor = weights[d]
            for index, (i, j) in enumerate(pairs):
                at = (slice(i * BLOCK, (i + 1) * BLOCK), slice(j * BLOCK, (j + 1) * BLOCK))
                system[at] = system[at] + factor * got[d, index * BLOCK:(index + 1) * BLOCK, :].astype(F32)
            extra = got[d, tail:tail + 16, :].astype(F32)
            both = extra[:8] + extra[8:]
            for b in range(blocks):
                at = (slice(0, 1), slice(b * BLOCK, (b + 1) * BLOCK))
                rhs_ref[at] = rhs_ref[at] + factor * both[b:b + 1]

    r_at = lax.broadcasted_iota(jnp.int32, (BLOCK, BLOCK), 0)
    c_at = lax.broadcasted_iota(jnp.int32, (BLOCK, BLOCK), 1)
    squares = jnp.zeros((BLOCK, BLOCK), F32)
    for i, j in pairs:
        rows_at, cols_at = slice(i * BLOCK, (i + 1) * BLOCK), slice(j * BLOCK, (j + 1) * BLOCK)
        piece = system[rows_at, cols_at]
        if i == j:
            piece = jnp.where(r_at <= c_at, piece, piece.T) + jnp.where(r_at == c_at, members - 1.0, 0.0)
            system[rows_at, cols_at] = piece
            squares = squares + piece * piece
        else:
            system[cols_at, rows_at] = piece.T
            squares = squares + 2.0 * (piece * piece)
    total = jnp.sum(jnp.sum(squares, axis=0, keepdims=True), axis=1, keepdims=True)
    norm = jnp.sqrt(total)
    inv_norm = 1.0 / norm

    def middle_of(part_value, start):
        shape = part_value.shape
        r = lax.broadcasted_iota(jnp.int32, shape, 0)
        c = lax.broadcasted_iota(jnp.int32, shape, 1) + start
        return jnp.where(r == c, 1.5, 0.0) - 0.5 * part_value

    chunks = [slice(start, start + part) for start in range(0, members, part)]

    def put(high_ref, low_ref, at, value):
        high, low = halves(value)
        high_ref[:, at] = high
        low_ref[:, at] = low

    def product(xh, xl, at):
        right_high = mh[:, at]
        return dot(xh[...], right_high) + dot(xl[...], right_high) + dot(xh[...], ml[:, at])

    for at in chunks:
        value = system[:, at] * inv_norm
        put(wh, wl, at, value)
        middle = middle_of(value, at.start)
        put(mh, ml, at, middle)
        put(zh, zl, at, middle)

    def advance():
        for at in chunks:
            put(th, tl, at, product(wh, wl, at))
        for at in chunks:
            system[:, at] = product(th, tl, at)
        for at in chunks:
            value = system[:, at]
            put(wh, wl, at, value)
            put(mh, ml, at, middle_of(value, at.start))

    advance()

    def sweep_body(sweep, carry):
        for at in chunks:
            put(th, tl, at, product(zh, zl, at))
        zh[...] = th[...]
        zl[...] = tl[...]
        advance()
        return carry

    lax.fori_loop(1, SWEEPS - 1, sweep_body, 0)
    for at in chunks:
        value = product(zh, zl, at)
        system[:, at] = value
        put(th, tl, at, value)

    def times_root(vec):
        high, low = halves(jnp.broadcast_to(vec, (16, members)))
        return (dot(high, th[...]) + dot(low, th[...]) + dot(high, tl[...]))[:1]

    mean = times_root(times_root(rhs_ref[:, :members])) * inv_norm
    scale = jnp.sqrt((members - 1.0) * inv_norm)

    own_state.wait()
    for k in range(len(flat)):
        state_copy(k).wait_recv()
    state_centre = add_up(state_in, cells)

    def deviation_body(i, carry):
        state_in[i] = (state_in[i].astype(F32) - state_centre).astype(BF16)
        return carry

    lax.fori_loop(0, grid.members, deviation_body, 0)
    deviation = state_in[...].reshape(members, cells)

    own_out = pltpu.make_async_copy(ana.at[mem], out_ref.at[:, columns_of(mem, cells)], local_sems.at[2])
    height = grid.slab * rows
    k = 0
    for dz, inner in steps:
        slab = (z + dz) % grid.slabs
        top = pl.multiple_of(slab * height, height)
        transform = (scale * system[pl.ds(top, height), :] + mean).astype(BF16)
        result = (state_centre + dot(transform, deviation)).astype(BF16)
        ana[pl.ds(slab * grid.slab, grid.slab)] = result.reshape(grid.slab, rows, cells)
        if dz == 0:
            own_out.start()
        for _ in inner:
            out_copy(k).start()
            k += 1

    own_out.wait()
    for k in range(len(flat)):
        out_copy(k).wait_recv()
    for k in range(len(flat)):
        obs_copy(k).wait_send()
        state_copy(k).wait_send()
        out_copy(k).wait_send()
    for d in range(4):

        @pl.when(neighbours[d][0])
        def _():
            gram_copy(d).wait_send()


def shards(grid, state_ens, obs_ens, obs_value, obs_class, loc_table, nbr_weight):
    rows = state_ens.shape[0]
    members = rows * grid.members
    wide, cells = obs_ens.shape[1] // grid.members, state_ens.shape[1] // grid.members
    blocks = members // BLOCK
    packed = blocks * (blocks + 1) // 2 * BLOCK + 16
    peers = grid.members - 1
    square = pltpu.VMEM((members, members), BF16)
    dma = pltpu.SemaphoreType.DMA
    vmem = pl.BlockSpec(memory_space=pltpu.VMEM)
    smem = pl.BlockSpec(memory_space=pltpu.SMEM)
    anywhere = pl.BlockSpec(memory_space=pl.ANY)
    return pl.pallas_call(
        functools.partial(kernel, grid),
        out_shape=jax.ShapeDtypeStruct(state_ens.shape, BF16),
        in_specs=[smem, smem, vmem, vmem, anywhere, anywhere],
        out_specs=anywhere,
        scratch_shapes=[
            pltpu.VMEM((grid.members, rows, wide), BF16),
            pltpu.VMEM((grid.members, rows, cells), BF16),
            pltpu.VMEM((1, wide), F32),
            pltpu.VMEM((1, wide), jnp.int32),
            pltpu.VMEM((grid.members, rows, wide), BF16),
            pltpu.VMEM((grid.members, rows, wide), BF16),
            pltpu.VMEM((packed, BLOCK), BF16),
            pltpu.VMEM((4, packed, BLOCK), BF16),
            pltpu.VMEM((members, members), F32),
        ]
        + [square] * 8
        + [
            pltpu.VMEM((grid.members, rows, cells), BF16),
            dma((3,)), dma((2, 2)), dma((peers,)), dma((peers,)), dma((peers,)), dma((peers,)),
            dma((4,)), dma((4,)), dma((peers,)), dma((peers,)),
        ],
        compiler_params=pltpu.CompilerParams(
            collective_id=0, has_side_effects=True, vmem_limit_bytes=48 * 1024 * 1024),
    )(nbr_weight, loc_table.astype(F32), obs_value[None, :], obs_class[None, :], state_ens, obs_ens)


def solution(mesh):
    grid = Grid(mesh.shape["grp"], mesh.shape["mem"])
    in_specs = (P("mem", "grp"), P("mem", "grp"), P(("grp", "mem")), P(("grp", "mem")), P(), P())
    return jax.shard_map(
        functools.partial(shards, grid), mesh=mesh, in_specs=in_specs, out_specs=P("mem", "grp"), check_vma=False)
```

time: 230 us -> 72.3 us (0.31)
  waiting for transfers between devices: 120 us -> 0 us
  Pallas kernels: 0 us -> 67.1 us
  starting transfers between devices: 35.4 us -> 0 us
  matrix products: 31 us -> 0 us
  blocking collectives: 24.9 us -> 0 us
  other arithmetic: 9.38 us -> 0.68 us
  between operations: 2.39 us -> 0.02 us
    ppermute x8 -> x0, waiting for transfers between devices: 97.9 us -> none  [shifted(): return lax.ppermute(array, axis, pairs)]
    pallas_call x0 -> x1, Pallas kernels: none -> 67.1 us  [shards(): pl.pallas_call(functools.partial(kernel, grid), out_shape=jax.ShapeDtypeS...]
    dot_general x19 -> x0, matrix products: 31 us -> none  [the longest x5 9.49 us: newton_root(): root_inv = jnp.dot(middle, root_inv, precision=lax.Precision.HIGHEST)]
    all_to_all x1 -> x0, blocking collectives: 24.9 us -> none  [shards(): lax.all_to_all(analysis_patch, 'mem', split_axis=0, concat_axis=1, tiled=...]
    all_to_all x2 -> x0, waiting for transfers between devices: 21.9 us -> none  [the longest x1 21.9 us: shards(): lax.all_to_all(obs_ens, 'mem', split_axis=1, concat_axis=0, tiled=True)]
    ppermute x8 -> x0, starting transfers between devices: 20.9 us -> none  [shifted(): return lax.ppermute(array, axis, pairs)]
    all_to_all x2 -> x0, starting transfers between devices: 14.5 us -> none  [the longest x1 7.52 us: shards(): lax.all_to_all(obs_ens, 'mem', split_axis=1, concat_axis=0, tiled=True)]
    reduce_sum x4 -> x0, other arithmetic: 4.91 us -> none  [the longest x1 4.52 us: newton_root(): norm_total = jnp.sqrt(jnp.sum(system * system))]
  transfers between devices with their start and end apart: 10 -> 0, of which waited for: 5 -> 0; matrix products, arithmetic and copies ran while one was open for 4% -> 0% of each run, Pallas kernels for 0% -> 0%
where the time goes in v1:
time: 72.3 us; the launch traced here: 71.6 us
  Pallas kernels  67.1 us (93%)
  local copies, waits for them, and re-layouts  3.75 us (5%)
    pallas_call x1, Pallas kernels, shards(): pl.pallas_call(functools.partial(kernel, grid), out_shape=jax.ShapeDtypeS...  67.1 us
    unnamed x11, local copies, waits for them, and re-layouts  3.75 us

profile of v1, /device:TPU:0, one launch (start us, length us, event | category | flops | bytes accessed | tf_op | source)
XLA Modules:
  0.0 71.6 jit_solution(3989182215436274813)
XLA Ops:
  0.0 0.0 copy-start.2
  0.0 0.0 copy-start.4
  0.0 0.7 convert_element_type.3.table
  0.7 0.0 copy-done.2
  0.7 0.0 copy-done.4
  0.7 0.0 copy-start
  0.7 1.2 %copy-done = bf16[32,16384]{1,0:T(8,128)(2,1)S(1)} copy-done((bf16[32,16384]{1,0:T(8,128)(2,1)S(1)}, bf16[32,16384]{1,0:T(8,128)(2,1)}, u32[]{:S(2)}) %copy-start) | copy-done | bytes 1048600
  1.9 0.0 copy-start.1
  1.9 1.0 %copy-done.1 = bf16[32,8192]{1,0:T(8,128)(2,1)S(1)} copy-done((bf16[32,8192]{1,0:T(8,128)(2,1)S(1)}, bf16[32,8192]{1,0:T(8,128)(2,1)}, u32[]{:S(2)}) %copy-start.1) | copy-done | bytes 524312
  3.0 0.0 copy-start.3
  3.0 0.7 copy-done.3
  3.7 67.1 %shard_map.64 = bf16[32,8192]{1,0:T(8,128)(2,1)S(1)} custom-call(f32[4]{0:T(128)S(1)} %copy-done.4, f32[16]{0:T(128)S(1)} %convert_element_type.3.table, f32[1,1024]{1,0:T(1,128)S(1)} %bitcast.2, s32[1,1024]{1,0:T(1,128)S(1)} %bitcast.3, bf16[32,8192]{1,0:T(8,128)(2,1)S(1)} %copy-done.1, bf16[32,16384]{1,0:T(8,128)(2,1)S(1)} %copy-done), custom_call_target="tpu_custom_call" | custom-call | tf_op jit(solution)/shard_map/pallas_call | solution.py:375
  70.8 0.8 %copy.8 = bf16[32,8192]{1,0:T(8,128)(2,1)} copy(bf16[32,8192]{1,0:T(8,128)(2,1)S(1)} %shard_map.64) | data formatting | bytes 1048576
Async XLA Ops:
  0.0 0.7 copy-start.2
  0.0 0.7 copy-start.4
  0.7 1.2 %copy-start = (bf16[32,16384]{1,0:T(8,128)(2,1)S(1)}, bf16[32,16384]{1,0:T(8,128)(2,1)}, u32[]{:S(2)}) copy-start(bf16[32,16384]{1,0:T(8,128)(2,1)} %obs_ref.1) | copy-start | bytes 3145732
  1.9 1.0 %copy-start.1 = (bf16[32,8192]{1,0:T(8,128)(2,1)S(1)}, bf16[32,8192]{1,0:T(8,128)(2,1)}, u32[]{:S(2)}) copy-start(bf16[32,8192]{1,0:T(8,128)(2,1)} %state_ref.1) | copy-start | bytes 1572868
  3.0 0.7 copy-start.3

commit v2 on v1

--- a/solution.py
+++ b/solution.py
@@ -48,12 +48,8 @@
 
     def peer(self, mem, dz, dy, dc):
         z, y, core = self.split(mem)
+        dz, dy, dc = dz % self.slabs, dy % self.rows, dc % CORES
         return self.join((z + dz) % self.slabs, (y + dy) % self.rows, (core + dc) % CORES)
-
-
-def halves(value):
-    high = value.astype(BF16)
-    return high, (value - high.astype(F32)).astype(BF16)
 
 
 def dot(a, b):
@@ -61,9 +57,9 @@
 
 
 def kernel(
-    grid, weights, table, value_ref, class_ref, state_ref, obs_ref, out_ref,
-    obs_in, state_in, value_in, class_in, spread, scaled, send, got, system,
-    wh, wl, mh, ml, zh, zl, th, tl, ana,
+    grid, classes, small_ref, value_ref, class_ref, state_ref, obs_ref, out_ref,
+    small, obs_in, state_in, value_in, class_in, spread, scaled, send, got, system,
+    wb, tb, zb_a, zb_b, mb_a, mb_b, wf, tf, zf, ana,
     local_sems, meta_sems, obs_send, obs_recv, state_send, state_recv,
     gram_send, gram_recv, out_send, out_recv,
 ):
@@ -147,7 +143,9 @@
     for k in range(len(flat)):
         obs_copy(k).start()
     own_obs.start()
-    own_state.start()
+    own_small = pltpu.make_async_copy(small_ref, small, local_sems.at[3])
+    own_small.start()
+    own_small.wait()
 
     @pl.when(meta_to != mem)
     def _():
@@ -160,20 +158,26 @@
             meta_local(k).wait()
 
     rates = jnp.zeros(class_in.shape, F32)
-    for code in range(table.shape[0]):
-        rates = jnp.where(class_in[...] == code, table[code], rates)
+    for code in range(classes):
+        rates = jnp.where(class_in[...] == code, small[code], rates)
+
+    def fold(block):
+        value = block.astype(F32)
+        if rows % 8:
+            return jnp.sum(value, axis=0, keepdims=True)
+        return jnp.sum(value.reshape(rows // 8, 8, value.shape[1]), axis=0)
 
     own_obs.wait()
+    total = fold(obs_in[mem])
     for k in range(len(flat)):
         obs_copy(k).wait_recv()
-
-    def add_up(source, width):
-        def body(i, total):
-            return total + jnp.sum(source[i].astype(F32), axis=0, keepdims=True)
-
-        return lax.fori_loop(0, grid.members, body, jnp.zeros((1, width), F32)) / members
-
-    centre = add_up(obs_in, wide)
+        dz, dy, dc = flat[k]
+        total = total + fold(obs_in[grid.peer(mem, -dz, -dy, -dc)])
+    centre = jnp.sum(total, axis=0, keepdims=True) / members
+
+    own_state.start()
+    for k in range(len(flat)):
+        state_copy(k).start()
 
     def spread_body(i, carry):
         block = (obs_in[i].astype(F32) - centre).astype(BF16)
@@ -225,9 +229,6 @@
         def _():
             gram_copy(d).start()
 
-    for k in range(len(flat)):
-        state_copy(k).start()
-
     rhs_ref = value_in
     rhs_ref[:, :members] = vector
     for d in (0, 1, 2, 3):
@@ -235,7 +236,7 @@
         @pl.when(neighbours[d][0])
         def _():
             gram_arrival(d).wait_recv()
-            factor = weights[d]
+            factor = small[classes + d]
             for index, (i, j) in enumerate(pairs):
                 at = (slice(i * BLOCK, (i + 1) * BLOCK), slice(j * BLOCK, (j + 1) * BLOCK))
                 system[at] = system[at] + factor * got[d, index * BLOCK:(index + 1) * BLOCK, :].astype(F32)
@@ -262,67 +263,99 @@
     norm = jnp.sqrt(total)
     inv_norm = 1.0 / norm
 
-    def middle_of(part_value, start):
-        shape = part_value.shape
-        r = lax.broadcasted_iota(jnp.int32, shape, 0)
-        c = lax.broadcasted_iota(jnp.int32, shape, 1) + start
-        return jnp.where(r == c, 1.5, 0.0) - 0.5 * part_value
+    def split_diagonal(value, start):
+        pieces, diagonal = [], None
+        for top in range(0, members, part):
+            piece = value[top:top + part]
+            if top == start:
+                same = (
+                    lax.broadcasted_iota(jnp.int32, piece.shape, 0)
+                    == lax.broadcasted_iota(jnp.int32, piece.shape, 1))
+                diagonal = jnp.sum(jnp.where(same, piece, 0.0), axis=0, keepdims=True)
+                piece = jnp.where(same, 0.0, piece)
+            pieces.append(piece)
+        return diagonal, pieces
 
     chunks = [slice(start, start + part) for start in range(0, members, part)]
 
-    def put(high_ref, low_ref, at, value):
-        high, low = halves(value)
-        high_ref[:, at] = high
-        low_ref[:, at] = low
-
-    def product(xh, xl, at):
-        right_high = mh[:, at]
-        return dot(xh[...], right_high) + dot(xl[...], right_high) + dot(xh[...], ml[:, at])
-
+    def put_middle(middle_ref, value, at):
+        diagonal, pieces = split_diagonal(value, at.start)
+        for n, piece in enumerate(pieces):
+            middle_ref[n * part:(n + 1) * part, at] = (-0.5 * piece).astype(BF16)
+        return 1.5 - 0.5 * diagonal, pieces
+
+    def product(x_full, x_half, middle_ref, diagonals, index):
+        at = chunks[index]
+        return x_full[:, at] * diagonals[index] + dot(x_half[...], middle_ref[:, at])
+
+    diagonals = []
     for at in chunks:
         value = system[:, at] * inv_norm
-        put(wh, wl, at, value)
-        middle = middle_of(value, at.start)
-        put(mh, ml, at, middle)
-        put(zh, zl, at, middle)
-
-    def advance():
-        for at in chunks:
-            put(th, tl, at, product(wh, wl, at))
-        for at in chunks:
-            system[:, at] = product(th, tl, at)
-        for at in chunks:
-            value = system[:, at]
-            put(wh, wl, at, value)
-            put(mh, ml, at, middle_of(value, at.start))
-
-    advance()
-
-    def sweep_body(sweep, carry):
-        for at in chunks:
-            put(th, tl, at, product(zh, zl, at))
-        zh[...] = th[...]
-        zl[...] = tl[...]
-        advance()
-        return carry
-
-    lax.fori_loop(1, SWEEPS - 1, sweep_body, 0)
-    for at in chunks:
-        value = product(zh, zl, at)
+        wf[:, at] = value
+        wb[:, at] = value.astype(BF16)
+        diagonal, pieces = put_middle(mb_a, value, at)
+        diagonals.append(diagonal)
+        for n, piece in enumerate(pieces):
+            where = slice(n * part, (n + 1) * part)
+            middle = -0.5 * piece
+            if where == at:
+                same = (
+                    lax.broadcasted_iota(jnp.int32, piece.shape, 0)
+                    == lax.broadcasted_iota(jnp.int32, piece.shape, 1))
+                middle = jnp.where(same, diagonal, middle)
+            zf[where, at] = middle
+            zb_a[where, at] = middle.astype(BF16)
+
+    def advance(middle, diagonals, later):
+        for index, at in enumerate(chunks):
+            value = product(wf, wb, middle, diagonals, index)
+            tf[:, at] = value
+            tb[:, at] = value.astype(BF16)
+        result = []
+        for index, at in enumerate(chunks):
+            value = product(tf, tb, middle, diagonals, index)
+            wf[:, at] = value
+            wb[:, at] = value.astype(BF16)
+            result.append(put_middle(later, value, at)[0])
+        return result
+
+    now, later = (zb_a, mb_a), (zb_b, mb_b)
+    diagonals = advance(mb_a, diagonals, mb_b)
+    now, later = (zb_a, mb_b), (zb_b, mb_a)
+    for sweep in range(1, SWEEPS - 1):
+        (z_now, m_now), (z_later, m_later) = now, later
+        for index, at in enumerate(chunks):
+            value = product(zf, z_now, m_now, diagonals, index)
+            zf[:, at] = value
+            z_later[:, at] = value.astype(BF16)
+        diagonals = advance(m_now, diagonals, m_later)
+        now, later = (z_later, m_later), (z_now, m_now)
+    root_diagonals = []
+    for index, at in enumerate(chunks):
+        value = product(zf, now[0], now[1], diagonals, index)
         system[:, at] = value
-        put(th, tl, at, value)
+        diagonal, pieces = split_diagonal(value, at.start)
+        root_diagonals.append(diagonal)
+        for n, piece in enumerate(pieces):
+            tb[n * part:(n + 1) * part, at] = piece.astype(BF16)
+    root_diagonal = jnp.concatenate(root_diagonals, axis=1)
 
     def times_root(vec):
-        high, low = halves(jnp.broadcast_to(vec, (16, members)))
-        return (dot(high, th[...]) + dot(low, th[...]) + dot(high, tl[...]))[:1]
+        high = vec.astype(BF16).astype(F32)
+        both = jnp.concatenate([high, vec - high, jnp.zeros((14, members), F32)], axis=0).astype(BF16)
+        result = dot(both, tb[...])
+        return vec * root_diagonal + result[0:1] + result[1:2]
 
     mean = times_root(times_root(rhs_ref[:, :members])) * inv_norm
     scale = jnp.sqrt((members - 1.0) * inv_norm)
 
     own_state.wait()
+    total = fold(state_in[mem])
     for k in range(len(flat)):
         state_copy(k).wait_recv()
-    state_centre = add_up(state_in, cells)
+        dz, dy, dc = flat[k]
+        total = total + fold(state_in[grid.peer(mem, -dz, -dy, -dc)])
+    state_centre = jnp.sum(total, axis=0, keepdims=True) / members
 
     def deviation_body(i, carry):
         state_in[i] = (state_in[i].astype(F32) - state_centre).astype(BF16)
@@ -367,17 +400,18 @@
     blocks = members // BLOCK
     packed = blocks * (blocks + 1) // 2 * BLOCK + 16
     peers = grid.members - 1
+    classes = loc_table.shape[0]
+    small = jnp.concatenate([loc_table.astype(F32), nbr_weight, jnp.zeros((-(classes + 4) % BLOCK,), F32)])
     square = pltpu.VMEM((members, members), BF16)
     dma = pltpu.SemaphoreType.DMA
-    vmem = pl.BlockSpec(memory_space=pltpu.VMEM)
-    smem = pl.BlockSpec(memory_space=pltpu.SMEM)
     anywhere = pl.BlockSpec(memory_space=pl.ANY)
     return pl.pallas_call(
-        functools.partial(kernel, grid),
+        functools.partial(kernel, grid, classes),
         out_shape=jax.ShapeDtypeStruct(state_ens.shape, BF16),
-        in_specs=[smem, smem, vmem, vmem, anywhere, anywhere],
+        in_specs=[anywhere] * 5,
         out_specs=anywhere,
         scratch_shapes=[
+            pltpu.SMEM(small.shape, F32),
             pltpu.VMEM((grid.members, rows, wide), BF16),
             pltpu.VMEM((grid.members, rows, cells), BF16),
             pltpu.VMEM((1, wide), F32),
@@ -388,15 +422,16 @@
             pltpu.VMEM((4, packed, BLOCK), BF16),
             pltpu.VMEM((members, members), F32),
         ]
-        + [square] * 8
+        + [square] * 6
+        + [pltpu.VMEM((members, members), F32)] * 3
         + [
             pltpu.VMEM((grid.members, rows, cells), BF16),
-            dma((3,)), dma((2, 2)), dma((peers,)), dma((peers,)), dma((peers,)), dma((peers,)),
+            dma((4,)), dma((2, 2)), dma((peers,)), dma((peers,)), dma((peers,)), dma((peers,)),
             dma((4,)), dma((4,)), dma((peers,)), dma((peers,)),
         ],
         compiler_params=pltpu.CompilerParams(
-            collective_id=0, has_side_effects=True, vmem_limit_bytes=48 * 1024 * 1024),
-    )(nbr_weight, loc_table.astype(F32), obs_value[None, :], obs_class[None, :], state_ens, obs_ens)
+            collective_id=0, has_side_effects=True, vmem_limit_bytes=62 * 1024 * 1024),
+    )(small, obs_value[None, :], obs_class[None, :], state_ens, obs_ens)
 
 
 def solution(mesh):

time: 72.3 us -> 68.2 us (0.943)
  Pallas kernels: 67.1 us -> 64.2 us
    pallas_call x1, Pallas kernels: 67.1 us -> 64.2 us  [shards(): pl.pallas_call(functools.partial(kernel, grid, classes), out_shape=jax.Sh...]
    unnamed x11 -> x5, local copies, waits for them, and re-layouts: 3.75 us -> 3.18 us
where the time goes in v2:
time: 68.2 us; the launch traced here: 68 us
  Pallas kernels  64.2 us (94%)
  local copies, waits for them, and re-layouts  3.18 us (5%)
    pallas_call x1, Pallas kernels, shards(): pl.pallas_call(functools.partial(kernel, grid, classes), out_shape=jax.Sh...  64.2 us
    unnamed x5, local copies, waits for them, and re-layouts  3.18 us

profile of v2, /device:TPU:0, one launch (start us, length us, event | category | flops | bytes accessed | tf_op | source)
XLA Modules:
  0.0 68.0 jit_solution(14604912546233528667)
XLA Ops:
  0.0 0.0 copy-start.1
  0.0 0.7 copy-done.1
  0.7 0.0 copy-start
  0.7 0.7 copy-done
  1.3 0.6 pad_maximum_fusion.small_ref
  1.9 64.2 %shard_map.64 = bf16[32,8192]{1,0:T(8,128)(2,1)} custom-call(f32[128]{0:T(128)} %pad_maximum_fusion.small_ref, f32[1,1024]{1,0:T(1,128)} %bitcast.2, s32[1,1024]{1,0:T(1,128)} %bitcast.3, bf16[32,8192]{1,0:T(8,128)(2,1)} %state_ref.1, bf16[32,16384]{1,0:T(8,128)(2,1)} %obs_ref.1), custom_call_target="tpu_custom_call" | custom-call | tf_op jit(solution)/shard_map/pallas_call | solution.py:408
  66.1 1.9 %copy.8 = bf16[32,8192]{1,0:T(8,128)(2,1)} copy(bf16[32,8192]{1,0:T(8,128)(2,1)} %shard_map.64) | data formatting | bytes 1048576
  (2 shorter events, 0.0 us)
Async XLA Ops:
  0.0 0.7 copy-start.1
  0.7 0.7 copy-start

commit v3 on v2

--- a/solution.py
+++ b/solution.py
@@ -57,8 +57,8 @@
 
 
 def kernel(
-    grid, classes, small_ref, value_ref, class_ref, state_ref, obs_ref, out_ref,
-    small, obs_in, state_in, value_in, class_in, spread, scaled, send, got, system,
+    grid, weights, table, value_ref, class_ref, state_ref, obs_ref, out_ref,
+    obs_in, state_in, value_in, class_in, spread, scaled, send, got, system,
     wb, tb, zb_a, zb_b, mb_a, mb_b, wf, tf, zf, ana,
     local_sems, meta_sems, obs_send, obs_recv, state_send, state_recv,
     gram_send, gram_recv, out_send, out_recv,
@@ -140,12 +140,10 @@
 
     own_obs = pltpu.make_async_copy(obs_ref.at[:, columns_of(mem, wide)], obs_in.at[mem], local_sems.at[0])
     own_state = pltpu.make_async_copy(state_ref.at[:, columns_of(mem, cells)], state_in.at[mem], local_sems.at[1])
-    for k in range(len(flat)):
+    turns = sorted(range(len(flat)), key=lambda k: sum(flat[n][0] == flat[k][0] for n in range(k)))
+    for k in turns:
         obs_copy(k).start()
     own_obs.start()
-    own_small = pltpu.make_async_copy(small_ref, small, local_sems.at[3])
-    own_small.start()
-    own_small.wait()
 
     @pl.when(meta_to != mem)
     def _():
@@ -158,8 +156,8 @@
             meta_local(k).wait()
 
     rates = jnp.zeros(class_in.shape, F32)
-    for code in range(classes):
-        rates = jnp.where(class_in[...] == code, small[code], rates)
+    for code in range(table.shape[0]):
+        rates = jnp.where(class_in[...] == code, table[code], rates)
 
     def fold(block):
         value = block.astype(F32)
@@ -169,15 +167,16 @@
 
     own_obs.wait()
     total = fold(obs_in[mem])
-    for k in range(len(flat)):
+    for k in turns:
         obs_copy(k).wait_recv()
         dz, dy, dc = flat[k]
         total = total + fold(obs_in[grid.peer(mem, -dz, -dy, -dc)])
     centre = jnp.sum(total, axis=0, keepdims=True) / members
 
     own_state.start()
-    for k in range(len(flat)):
-        state_copy(k).start()
+    for k in turns:
+        if flat[k][1] == 0:
+            state_copy(k).start()
 
     def spread_body(i, carry):
         block = (obs_in[i].astype(F32) - centre).astype(BF16)
@@ -189,27 +188,30 @@
     innovation = (rates * (value_in[...] - centre)).astype(BF16)
 
     blocks = members // BLOCK
-    pairs = [(i, j) for i in range(blocks) for j in range(i, blocks)]
+    pairs = [(i, j) for i in range(blocks) for j in range(i + 1)]
     all_spread = spread[...].reshape(members, wide)
     all_scaled = scaled[...].reshape(members, wide)
-    vector = lax.dot_general(
-        jnp.broadcast_to(innovation, (16, wide)), all_spread, (((1,), (1,)), ((), ())), preferred_element_type=F32)[:1]
+    left = jnp.concatenate([all_scaled, jnp.broadcast_to(innovation, (16, wide))], axis=0)
+    part = 2 * BLOCK
+    vectors = []
+    for start in range(0, members, part):
+        stripe = lax.dot_general(
+            left[start:], all_spread[start:start + part], (((1,), (1,)), ((), ())), preferred_element_type=F32)
+        vectors.append(stripe[members - start:members - start + 1])
+        system[start:, start:start + part] = stripe[:members - start]
+        for index, (i, j) in enumerate(pairs):
+            if start <= j * BLOCK < start + part:
+                at = j * BLOCK - start
+                piece = stripe[i * BLOCK - start:(i + 1) * BLOCK - start, at:at + BLOCK]
+                send[index * BLOCK:(index + 1) * BLOCK, :] = piece.astype(BF16)
+
+    vector = jnp.concatenate(vectors, axis=1)
     pieces = jnp.concatenate(
         [vector[:, b * BLOCK:(b + 1) * BLOCK] for b in range(blocks)]
         + [jnp.zeros((8 - blocks, BLOCK), F32)], axis=0)
     pieces_high = pieces.astype(BF16).astype(F32)
     tail = len(pairs) * BLOCK
     send[tail:tail + 16, :] = jnp.concatenate([pieces_high, pieces - pieces_high], axis=0).astype(BF16)
-    part = 2 * BLOCK
-    for start in range(0, members, part):
-        stripe = lax.dot_general(
-            all_spread[start:start + part], all_scaled[start:], (((1,), (1,)), ((), ())), preferred_element_type=F32)
-        system[start:start + part, start:] = stripe
-        for index, (i, j) in enumerate(pairs):
-            if start <= i * BLOCK < start + part:
-                at = i * BLOCK - start
-                piece = stripe[at:at + BLOCK, j * BLOCK - start:(j + 1) * BLOCK - start]
-                send[index * BLOCK:(index + 1) * BLOCK, :] = piece.astype(BF16)
 
     opposite = (1, 0, 3, 2)
 
@@ -236,7 +238,7 @@
         @pl.when(neighbours[d][0])
         def _():
             gram_arrival(d).wait_recv()
-            factor = small[classes + d]
+            factor = weights[d]
             for index, (i, j) in enumerate(pairs):
                 at = (slice(i * BLOCK, (i + 1) * BLOCK), slice(j * BLOCK, (j + 1) * BLOCK))
                 system[at] = system[at] + factor * got[d, index * BLOCK:(index + 1) * BLOCK, :].astype(F32)
@@ -246,6 +248,10 @@
                 at = (slice(0, 1), slice(b * BLOCK, (b + 1) * BLOCK))
                 rhs_ref[at] = rhs_ref[at] + factor * both[b:b + 1]
 
+    for k in turns:
+        if flat[k][1] != 0:
+            state_copy(k).start()
+
     r_at = lax.broadcasted_iota(jnp.int32, (BLOCK, BLOCK), 0)
     c_at = lax.broadcasted_iota(jnp.int32, (BLOCK, BLOCK), 1)
     squares = jnp.zeros((BLOCK, BLOCK), F32)
@@ -253,7 +259,7 @@
         rows_at, cols_at = slice(i * BLOCK, (i + 1) * BLOCK), slice(j * BLOCK, (j + 1) * BLOCK)
         piece = system[rows_at, cols_at]
         if i == j:
-            piece = jnp.where(r_at <= c_at, piece, piece.T) + jnp.where(r_at == c_at, members - 1.0, 0.0)
+            piece = jnp.where(r_at >= c_at, piece, piece.T) + jnp.where(r_at == c_at, members - 1.0, 0.0)
             system[rows_at, cols_at] = piece
             squares = squares + piece * piece
         else:
@@ -400,18 +406,16 @@
     blocks = members // BLOCK
     packed = blocks * (blocks + 1) // 2 * BLOCK + 16
     peers = grid.members - 1
-    classes = loc_table.shape[0]
-    small = jnp.concatenate([loc_table.astype(F32), nbr_weight, jnp.zeros((-(classes + 4) % BLOCK,), F32)])
     square = pltpu.VMEM((members, members), BF16)
     dma = pltpu.SemaphoreType.DMA
+    smem = pl.BlockSpec(memory_space=pltpu.SMEM)
     anywhere = pl.BlockSpec(memory_space=pl.ANY)
     return pl.pallas_call(
-        functools.partial(kernel, grid, classes),
+        functools.partial(kernel, grid),
         out_shape=jax.ShapeDtypeStruct(state_ens.shape, BF16),
-        in_specs=[anywhere] * 5,
+        in_specs=[smem] * 2 + [anywhere] * 4,
         out_specs=anywhere,
         scratch_shapes=[
-            pltpu.SMEM(small.shape, F32),
             pltpu.VMEM((grid.members, rows, wide), BF16),
             pltpu.VMEM((grid.members, rows, cells), BF16),
             pltpu.VMEM((1, wide), F32),
@@ -426,12 +430,12 @@
         + [pltpu.VMEM((members, members), F32)] * 3
         + [
             pltpu.VMEM((grid.members, rows, cells), BF16),
-            dma((4,)), dma((2, 2)), dma((peers,)), dma((peers,)), dma((peers,)), dma((peers,)),
+            dma((3,)), dma((2, 2)), dma((peers,)), dma((peers,)), dma((peers,)), dma((peers,)),
             dma((4,)), dma((4,)), dma((peers,)), dma((peers,)),
         ],
         compiler_params=pltpu.CompilerParams(
             collective_id=0, has_side_effects=True, vmem_limit_bytes=62 * 1024 * 1024),
-    )(small, obs_value[None, :], obs_class[None, :], state_ens, obs_ens)
+    )(nbr_weight, loc_table.astype(F32), obs_value[None, :], obs_class[None, :], state_ens, obs_ens)
 
 
 def solution(mesh):

time: 68.2 us -> 66.3 us (0.972); the launches traced: 68 us -> 65.4 us
  Pallas kernels: 64.2 us -> 62.3 us
    pallas_call x1, Pallas kernels: 64.2 us -> 62.3 us  [shards(): pl.pallas_call(functools.partial(kernel, grid), out_shape=jax.ShapeDtypeS...]
    unnamed x5 -> x3, local copies, waits for them, and re-layouts: 3.18 us -> 2.52 us
where the time goes in v3:
time: 66.3 us; the launch traced here: 65.4 us
  Pallas kernels  62.3 us (94%)
  local copies, waits for them, and re-layouts  2.52 us (4%)
    pallas_call x1, Pallas kernels, shards(): pl.pallas_call(functools.partial(kernel, grid), out_shape=jax.ShapeDtypeS...  62.3 us
    unnamed x3, local copies, waits for them, and re-layouts  2.52 us

profile of v3, /device:TPU:0, one launch (start us, length us, event | category | flops | bytes accessed | tf_op | source)
XLA Modules:
  0.0 65.4 jit_solution(2573226039525932518)
XLA Ops:
  0.0 0.0 copy-start
  0.0 0.7 copy-done
  0.7 0.5 convert_element_type.3.table
  1.2 62.3 %shard_map.64 = bf16[32,8192]{1,0:T(8,128)(2,1)} custom-call(f32[4]{0:T(128)} %weights.1, f32[16]{0:T(128)} %convert_element_type.3.table, f32[1,1024]{1,0:T(1,128)} %bitcast.2, s32[1,1024]{1,0:T(1,128)} %bitcast.3, bf16[32,8192]{1,0:T(8,128)(2,1)} %state_ref.1, bf16[32,16384]{1,0:T(8,128)(2,1)} %obs_ref.1), custom_call_target="tpu_custom_call" | custom-call | tf_op jit(solution)/shard_map/pallas_call | solution.py:413
  63.5 1.9 %copy.8 = bf16[32,8192]{1,0:T(8,128)(2,1)} copy(bf16[32,8192]{1,0:T(8,128)(2,1)} %shard_map.64) | data formatting | bytes 1048576
Async XLA Ops:
  0.0 0.7 %copy-start = (bf16[16]{0:T(256)(128)(2,1)S(1)}, bf16[16]{0:T(256)(128)(2,1)}, u32[]{:S(2)}) copy-start(bf16[16]{0:T(256)(128)(2,1)} %param.10) | copy-start | bytes 100

commit v4 on v3

--- a/solution.py
+++ b/solution.py
@@ -10,6 +10,7 @@
 ROW_PATCHES = 8
 CORES = 2
 BLOCK = 128
+PARTS = 2
 BF16 = jnp.bfloat16
 F32 = jnp.float32
 MESH = pl.DeviceIdType.MESH
@@ -65,8 +66,9 @@
 ):
     group, mem = lax.axis_index("grp"), lax.axis_index("mem")
     members = system.shape[0]
-    rows = obs_in.shape[1]
-    wide, cells = obs_in.shape[2], state_in.shape[2]
+    rows = obs_in.shape[2]
+    half, cells = obs_in.shape[3], state_in.shape[2]
+    wide = PARTS * half
     z, y, core = grid.split(mem)
     row, column = grid.flip(group, y), z * CORES + core
     all_row = group * grid.rows + row
@@ -99,11 +101,17 @@
     def columns_of(device, width):
         return pl.ds(pl.multiple_of(grid.patch(group, device) * width, BLOCK), width)
 
-    def obs_copy(k):
+    def obs_columns(device, h):
+        return pl.ds(pl.multiple_of(grid.patch(group, device) * wide + h * half, BLOCK), half)
+
+    def obs_copy(k, h):
         to = grid.peer(mem, *flat[k])
         return pltpu.make_async_remote_copy(
-            src_ref=obs_ref.at[:, columns_of(to, wide)], dst_ref=obs_in.at[mem],
-            send_sem=obs_send.at[k], recv_sem=obs_recv.at[k], device_id=(group, to), device_id_type=MESH)
+            src_ref=obs_ref.at[:, obs_columns(to, h)], dst_ref=obs_in.at[h, mem],
+            send_sem=obs_send.at[h, k], recv_sem=obs_recv.at[h, k], device_id=(group, to), device_id_type=MESH)
+
+    def own_obs(h):
+        return pltpu.make_async_copy(obs_ref.at[:, obs_columns(mem, h)], obs_in.at[h, mem], local_sems.at[2 + h])
 
     def state_copy(k):
         to = grid.peer(mem, *flat[k])
@@ -138,12 +146,12 @@
         for k in range(2):
             meta_local(k).start()
 
-    own_obs = pltpu.make_async_copy(obs_ref.at[:, columns_of(mem, wide)], obs_in.at[mem], local_sems.at[0])
     own_state = pltpu.make_async_copy(state_ref.at[:, columns_of(mem, cells)], state_in.at[mem], local_sems.at[1])
     turns = sorted(range(len(flat)), key=lambda k: sum(flat[n][0] == flat[k][0] for n in range(k)))
-    for k in turns:
-        obs_copy(k).start()
-    own_obs.start()
+    for h in range(PARTS):
+        for k in turns:
+            obs_copy(k, h).start()
+        own_obs(h).start()
 
     @pl.when(meta_to != mem)
     def _():
@@ -165,45 +173,52 @@
             return jnp.sum(value, axis=0, keepdims=True)
         return jnp.sum(value.reshape(rows // 8, 8, value.shape[1]), axis=0)
 
-    own_obs.wait()
-    total = fold(obs_in[mem])
-    for k in turns:
-        obs_copy(k).wait_recv()
-        dz, dy, dc = flat[k]
-        total = total + fold(obs_in[grid.peer(mem, -dz, -dy, -dc)])
-    centre = jnp.sum(total, axis=0, keepdims=True) / members
-
-    own_state.start()
-    for k in turns:
-        if flat[k][1] == 0:
-            state_copy(k).start()
-
-    def spread_body(i, carry):
-        block = (obs_in[i].astype(F32) - centre).astype(BF16)
-        spread[i] = block
-        scaled[i] = (block.astype(F32) * rates).astype(BF16)
-        return carry
-
-    lax.fori_loop(0, grid.members, spread_body, 0)
-    innovation = (rates * (value_in[...] - centre)).astype(BF16)
-
     blocks = members // BLOCK
     pairs = [(i, j) for i in range(blocks) for j in range(i + 1)]
-    all_spread = spread[...].reshape(members, wide)
-    all_scaled = scaled[...].reshape(members, wide)
-    left = jnp.concatenate([all_scaled, jnp.broadcast_to(innovation, (16, wide))], axis=0)
     part = 2 * BLOCK
-    vectors = []
-    for start in range(0, members, part):
-        stripe = lax.dot_general(
-            left[start:], all_spread[start:start + part], (((1,), (1,)), ((), ())), preferred_element_type=F32)
-        vectors.append(stripe[members - start:members - start + 1])
-        system[start:, start:start + part] = stripe[:members - start]
-        for index, (i, j) in enumerate(pairs):
-            if start <= j * BLOCK < start + part:
-                at = j * BLOCK - start
-                piece = stripe[i * BLOCK - start:(i + 1) * BLOCK - start, at:at + BLOCK]
-                send[index * BLOCK:(index + 1) * BLOCK, :] = piece.astype(BF16)
+    vectors = [0.0] * (members // part)
+    for h in range(PARTS):
+        at_h = slice(h * half, (h + 1) * half)
+        own_obs(h).wait()
+        total = fold(obs_in[h, mem])
+        for k in turns:
+            obs_copy(k, h).wait_recv()
+            dz, dy, dc = flat[k]
+            total = total + fold(obs_in[h, grid.peer(mem, -dz, -dy, -dc)])
+        centre = jnp.sum(total, axis=0, keepdims=True) / members
+
+        if h == PARTS - 1:
+            own_state.start()
+            for k in turns:
+                if flat[k][1] == 0:
+                    state_copy(k).start()
+
+        def spread_body(i, carry):
+            block = (obs_in[h, i].astype(F32) - centre).astype(BF16)
+            spread[h, i] = block
+            scaled[h, i] = (block.astype(F32) * rates[:, at_h]).astype(BF16)
+            return carry
+
+        lax.fori_loop(0, grid.members, spread_body, 0)
+        innovation = (rates[:, at_h] * (value_in[:, at_h] - centre)).astype(BF16)
+        all_spread = spread[h].reshape(members, half)
+        all_scaled = scaled[h].reshape(members, half)
+        left = jnp.concatenate([all_scaled, jnp.broadcast_to(innovation, (16, half))], axis=0)
+        for n, start in enumerate(range(0, members, part)):
+            stripe = lax.dot_general(
+                left[start:], all_spread[start:start + part], (((1,), (1,)), ((), ())), preferred_element_type=F32)
+            vectors[n] = vectors[n] + stripe[members - start:members - start + 1]
+            stripe = stripe[:members - start]
+            if h > 0:
+                stripe = stripe + system[start:, start:start + part]
+            system[start:, start:start + part] = stripe
+            if h < PARTS - 1:
+                continue
+            for index, (i, j) in enumerate(pairs):
+                if start <= j * BLOCK < start + part:
+                    at = j * BLOCK - start
+                    piece = stripe[i * BLOCK - start:(i + 1) * BLOCK - start, at:at + BLOCK]
+                    send[index * BLOCK:(index + 1) * BLOCK, :] = piece.astype(BF16)
 
     vector = jnp.concatenate(vectors, axis=1)
     pieces = jnp.concatenate(
@@ -370,7 +385,7 @@
     lax.fori_loop(0, grid.members, deviation_body, 0)
     deviation = state_in[...].reshape(members, cells)
 
-    own_out = pltpu.make_async_copy(ana.at[mem], out_ref.at[:, columns_of(mem, cells)], local_sems.at[2])
+    own_out = pltpu.make_async_copy(ana.at[mem], out_ref.at[:, columns_of(mem, cells)], local_sems.at[0])
     height = grid.slab * rows
     k = 0
     for dz, inner in steps:
@@ -389,7 +404,8 @@
     for k in range(len(flat)):
         out_copy(k).wait_recv()
     for k in range(len(flat)):
-        obs_copy(k).wait_send()
+        for h in range(PARTS):
+            obs_copy(k, h).wait_send()
         state_copy(k).wait_send()
         out_copy(k).wait_send()
     for d in range(4):
@@ -412,16 +428,16 @@
     anywhere = pl.BlockSpec(memory_space=pl.ANY)
     return pl.pallas_call(
         functools.partial(kernel, grid),
-        out_shape=jax.ShapeDtypeStruct(state_ens.shape, BF16),
+        out_shape=pltpu.VMEM(state_ens.shape, BF16),
         in_specs=[smem] * 2 + [anywhere] * 4,
-        out_specs=anywhere,
+        out_specs=pl.BlockSpec(memory_space=pltpu.VMEM),
         scratch_shapes=[
-            pltpu.VMEM((grid.members, rows, wide), BF16),
+            pltpu.VMEM((PARTS, grid.members, rows, wide // PARTS), BF16),
             pltpu.VMEM((grid.members, rows, cells), BF16),
             pltpu.VMEM((1, wide), F32),
             pltpu.VMEM((1, wide), jnp.int32),
-            pltpu.VMEM((grid.members, rows, wide), BF16),
-            pltpu.VMEM((grid.members, rows, wide), BF16),
+            pltpu.VMEM((PARTS, grid.members, rows, wide // PARTS), BF16),
+            pltpu.VMEM((PARTS, grid.members, rows, wide // PARTS), BF16),
             pltpu.VMEM((packed, BLOCK), BF16),
             pltpu.VMEM((4, packed, BLOCK), BF16),
             pltpu.VMEM((members, members), F32),
@@ -430,11 +446,11 @@
         + [pltpu.VMEM((members, members), F32)] * 3
         + [
             pltpu.VMEM((grid.members, rows, cells), BF16),
-            dma((3,)), dma((2, 2)), dma((peers,)), dma((peers,)), dma((peers,)), dma((peers,)),
+            dma((2 + PARTS,)), dma((2, 2)), dma((PARTS, peers)), dma((PARTS, peers)), dma((peers,)), dma((peers,)),
             dma((4,)), dma((4,)), dma((peers,)), dma((peers,)),
         ],
         compiler_params=pltpu.CompilerParams(
-            collective_id=0, has_side_effects=True, vmem_limit_bytes=62 * 1024 * 1024),
+            collective_id=0, has_side_effects=True, vmem_limit_bytes=60 * 1024 * 1024),
     )(nbr_weight, loc_table.astype(F32), obs_value[None, :], obs_class[None, :], state_ens, obs_ens)
 
 

time: 66.3 us -> 64.9 us (0.979)
  local copies, waits for them, and re-layouts: 2.52 us -> 1.45 us
    unnamed x3, local copies, waits for them, and re-layouts: 2.52 us -> 1.45 us
where the time goes in v4:
time: 64.9 us; the launch traced here: 63.9 us
  Pallas kernels  61.9 us (95%)
  local copies, waits for them, and re-layouts  1.45 us (2%)
    pallas_call x1, Pallas kernels, shards(): pl.pallas_call(functools.partial(kernel, grid), out_shape=pltpu.VMEM(stat...  61.9 us
    unnamed x3, local copies, waits for them, and re-layouts  1.45 us

profile of v4, /device:TPU:0, one launch (start us, length us, event | category | flops | bytes accessed | tf_op | source)
XLA Modules:
  0.0 63.9 jit_solution(2266403383202741468)
XLA Ops:
  0.0 0.0 copy-start
  0.0 0.7 %copy-done = bf16[16]{0:T(256)(128)(2,1)S(1)} copy-done((bf16[16]{0:T(256)(128)(2,1)S(1)}, bf16[16]{0:T(256)(128)(2,1)}, u32[]{:S(2)}) %copy-start) | copy-done | bytes 56
  0.7 0.5 convert_element_type.3.table
  1.2 61.9 %shard_map.64 = bf16[32,8192]{1,0:T(8,128)(2,1)S(1)} custom-call(f32[4]{0:T(128)} %weights.1, f32[16]{0:T(128)} %convert_element_type.3.table, f32[1,1024]{1,0:T(1,128)} %bitcast.2, s32[1,1024]{1,0:T(1,128)} %bitcast.3, bf16[32,8192]{1,0:T(8,128)(2,1)} %state_ref.1, bf16[32,16384]{1,0:T(8,128)(2,1)} %obs_ref.1), custom_call_target="tpu_custom_call" | custom-call | tf_op jit(solution)/shard_map/pallas_call | solution.py:429
  63.1 0.8 %copy.8 = bf16[32,8192]{1,0:T(8,128)(2,1)} copy(bf16[32,8192]{1,0:T(8,128)(2,1)S(1)} %shard_map.64) | data formatting | bytes 1048576
Async XLA Ops:
  0.0 0.7 %copy-start = (bf16[16]{0:T(256)(128)(2,1)S(1)}, bf16[16]{0:T(256)(128)(2,1)}, u32[]{:S(2)}) copy-start(bf16[16]{0:T(256)(128)(2,1)} %param.10) | copy-start | bytes 100
